TPU v7x, 256 devices: a whole 4x4x8 slice. The times are simulated.
256 devices in a mesh: fsdp: 32 (over y_hi, z, core), mp: 8 (over y_lo, x).
Axes of the slice: x: 4, y: 4 (y_hi: 2, y_lo: 2; y = y_hi * 2 + y_lo), z: 8, core: 2. Of those that a mesh axis runs over, the one named last changes fastest.
Arguments:
- tokens: bfloat16 [16384, 3072], P('fsdp', 'mp'), may hold values from -6 to 6
- ln_gain: float32 [3072], replicated, may hold values from 0.1 to 1.9
- w_qkv: bfloat16 [3072, 3, 3072], P('fsdp', None, 'mp'), may hold values from -0.109375 to 0.109375
- w_up: bfloat16 [3072, 12288], P('fsdp', 'mp'), may hold values from -0.109375 to 0.109375
- q_gain: float32 [24, 128], P('mp'), may hold values from 0.4 to 16
- k_gain: float32 [24, 128], P('mp'), may hold values from 0.4 to 16
- w_proj: bfloat16 [3072, 3072], P('mp', 'fsdp'), may hold values from -0.109375 to 0.109375
- w_down: bfloat16 [12288, 3072], P('mp', 'fsdp'), may hold values from -0.0546875 to 0.0546875
Outputs:
- block_out: bfloat16 [16384, 3072], P('fsdp', 'mp')
All inputs are finite; a program needn't handle non-finite values.
Results may differ from a plain program's by a relative error of at most 0.015.
Values may be sent and summed in bfloat16 or wider, within the bound.
No kernel may reach another device: no remote copies, remote signals or barrier semaphores. Data moves between devices by JAX's collectives and lax.ppermute only.
A program may use at most 128 MiB of HBM per device.

v0:
```python
import jax
import jax.numpy as jnp
from jax import lax
from jax.sharding import PartitionSpec as P

HD = 128
PATCHES = 256


def layer_norm(values, gain):
    mean = jnp.mean(values, axis=-1, keepdims=True)
    centred = values - mean
    variance = jnp.mean(centred * centred, axis=-1, keepdims=True)
    return centred * lax.rsqrt(variance + 1e-06) * gain


def local(tokens, ln_gain, w_qkv, w_up, q_gain, k_gain, w_proj, w_down):
    rows = tokens.astype(jnp.float32)
    panels = lax.all_gather(tokens, "mp", axis=1, tiled=True)
    normed = layer_norm(panels.astype(jnp.float32), ln_gain).astype(jnp.bfloat16)
    tok_count = panels.shape[0]
    head_cols = w_qkv.shape[2]
    heads_here = q_gain.shape[0]
    columns = normed
    projected = jnp.einsum(
        "td,dca->cta",
        columns,
        lax.all_gather(w_qkv, "fsdp", axis=0, tiled=True),
        preferred_element_type=jnp.float32,
    )
    columns = normed
    hidden_pre = jnp.dot(
        columns,
        lax.all_gather(w_up, "fsdp", axis=0, tiled=True),
        preferred_element_type=jnp.float32,
    )
    images = tok_count // PATCHES
    queries = layer_norm(projected[0].reshape(tok_count, heads_here, HD), q_gain).astype(
        jnp.bfloat16
    )
    keys = layer_norm(projected[1].reshape(tok_count, heads_here, HD), k_gain).astype(jnp.bfloat16)
    values = projected[2].reshape(tok_count, heads_here, HD).astype(jnp.bfloat16)
    queries = queries.reshape(images, PATCHES, heads_here, HD)
    keys = keys.reshape(images, PATCHES, heads_here, HD)
    values = values.reshape(images, PATCHES, heads_here, HD)
    scores = jnp.einsum(
        "iqhd,ikhd->ihqk", queries, keys, preferred_element_type=jnp.float32
    ) * HD ** (-0.5)
    scores = scores - jnp.max(scores, axis=-1, keepdims=True)
    weights = jnp.exp(scores)
    probs = (weights / jnp.sum(weights, axis=-1, keepdims=True)).astype(jnp.bfloat16)
    attended = jnp.einsum("ihqk,ikhd->iqhd", probs, values, preferred_element_type=jnp.float32)
    attended = attended.astype(jnp.bfloat16).reshape(tok_count, head_cols)
    activated = jax.nn.gelu(hidden_pre, approximate=False).astype(jnp.bfloat16)
    joined = jnp.concatenate([attended, activated], axis=1)
    out_rows = jnp.concatenate([w_proj, w_down], axis=0)
    terms = jnp.dot(
        joined,
        lax.all_gather(out_rows, "fsdp", axis=1, tiled=True),
        preferred_element_type=jnp.float32,
    )
    branches = lax.psum_scatter(
        terms.astype(jnp.bfloat16), "mp", scatter_dimension=1, tiled=True
    ).astype(jnp.float32)
    return (rows + branches).astype(jnp.bfloat16)


def solution(mesh):
    return jax.shard_map(
        local,
        mesh=mesh,
        in_specs=(
            P("fsdp", "mp"),
            P(),
            P("fsdp", None, "mp"),
            P("fsdp", "mp"),
            P("mp", None),
            P("mp", None),
            P("mp", "fsdp"),
            P("mp", "fsdp"),
        ),
        out_specs=P("fsdp", "mp"),
        check_vma=False,
    )
```

profile of v0, /device:TPU:16, one launch (start us, length us, event | category | flops | bytes accessed | tf_op | source)
XLA Modules:
  0.0 442.9 jit_solution(9874323339056634147)
XLA Ops:
  6.5 0.0 all-gather.5.cloned.1.call-start
  6.5 0.7 all-gather.5.cloned.1.call-update
  7.3 0.0 all-gather.7.cloned.1.call-start
  7.3 0.7 all-gather.7.cloned.1.call-update
  8.0 0.0 all-gather.9.cloned.1.call-start
  8.1 0.7 all-gather.9.cloned.1.call-update
  8.7 0.0 all-gather.11.cloned.1.call-start
  8.8 1.8 pad_maximum_fusion
  10.6 0.0 all-gather.11.cloned.1.call-update
  10.6 0.0 reduce-scatter.4.cloned.1.call-start
  10.6 47.8 %all-gather.5.cloned.1.call-done = bf16[512,3072]{1,0:T(8,128)(2,1)} async-done(((bf16[512,384]{1,0:T(8,128)(2,1)}), bf16[512,3072]{1,0:T(8,128)(2,1)}) %all-gather.5.cloned.1.call-update) | async-done | bytes 3145744 | tf_op jit(solution)/shard_map/all_gather | solution.py:19
  58.4 2.5 convert_reduce_fusion
  61.0 0.3 copy-done
  61.3 1.0 fusion.3
  62.2 0.0 copy-start.5
  62.2 93.3 %all-gather.7.cloned.1.call-done = bf16[3072,3,384]{2,0,1:T(8,128)(2,1)} async-done(((bf16[96,3,384]{2,0,1:T(8,128)(2,1)}), bf16[3072,3,384]{2,0,1:T(8,128)(2,1)}) %all-gather.7.cloned.1.call-update) | async-done | bytes 7077904 | tf_op jit(solution)/shard_map/all_gather | solution.py:28
  155.6 0.0 copy-done.3
  155.6 0.0 copy-done.5
  155.6 0.0 copy-done.7
  155.6 7.1 %fusion.21 = f32[3,512,384]{1,2,0:T(8,128)S(1)} fusion(bf16[3072,3,384]{2,0,1:T(8,128)(2,1)} %all-gather.7.cloned.1.call-done, bf16[512,3072]{1,0:T(8,128)(2,1)S(1)} %copy-done, f32[3072]{0:T(1024)S(1)} %copy-done.7, f32[512]{0:T(512)S(1)} %add_rsqrt_fusion.2, f32[512]{0:T(512)S(1)} %broadcast_multiply_fusion.2), kind=kOutput, calls=%fused_computation.33 | convolution fusion | flops 3631742976 | bytes 12599296 | tf_op jit(solution)/shard_map/td,dca->cta/dot_general | solution.py:25
  162.7 0.1 slice.17
  162.7 1.3 fusion.41
  164.0 2.5 reshape_squeeze.11
  166.5 2.5 reshape_squeeze.13
  169.1 1.2 reduce_sum.65
  170.3 1.2 reduce_sum.67
  171.5 2.3 copy.19
  173.8 2.1 copy.20
  175.9 0.8 convert_element_type.46
  176.8 1.2 multiply_reduce_fusion.1
  178.0 1.2 multiply_reduce_fusion
  179.3 2.4 convolution_multiply_fusion
  181.8 0.0 copy-start.1
  181.8 1.2 copy-done.1
  182.9 0.3 fusion.42
  183.3 2.6 fusion.26
  185.8 1.0 copy.26
  186.9 1.1 copy.34
  188.0 72.3 %all-gather.9.cloned.1.call-done = bf16[3072,1536]{1,0:T(8,128)(2,1)} async-done(((bf16[96,1536]{1,0:T(8,128)(2,1)}), bf16[3072,1536]{1,0:T(8,128)(2,1)}) %all-gather.9.cloned.1.call-update) | async-done | bytes 9437200 | tf_op jit(solution)/shard_map/all_gather | solution.py:34
  260.3 0.0 copy-done.6
  260.3 14.9 %fusion.8 = bf16[512,1536]{1,0:T(8,128)(2,1)} fusion(bf16[3072,1536]{1,0:T(8,128)(2,1)} %all-gather.9.cloned.1.call-done, bf16[512,3072]{1,0:T(8,128)(2,1)S(1)} %copy-done, f32[3072]{0:T(1024)} %param.9, f32[512]{0:T(512)S(1)} %copy-done.6, f32[512]{0:T(512)S(1)} %copy-done.4), kind=kOutput, calls=%fused_computation.12 | convolution fusion | flops 4890820608 | bytes 14172160 | tf_op jit(solution)/shard_map/dot_general | solution.py:32
  275.2 98.2 %all-gather.11.cloned.1.call-done = bf16[1920,3072]{0,1:T(8,128)(2,1)} async-done(((bf16[1920,96]{0,1:T(8,128)(2,1)}), bf16[1920,3072]{0,1:T(8,128)(2,1)}) %all-gather.11.cloned.1.call-update) | async-done | bytes 11796496 | tf_op jit(solution)/shard_map/all_gather | solution.py:59
  373.5 10.1 %convolution_convert_fusion = bf16[512,3072]{1,0:T(8,128)(2,1)S(1)} fusion(bf16[1920,3072]{0,1:T(8,128)(2,1)} %all-gather.11.cloned.1.call-done, bf16[512,1536]{1,0:T(8,128)(2,1)} %fusion.8, bf16[512,384]{1,0:T(8,128)(2,1)S(1)} %bitcast.39), kind=kOutput, calls=%fused_computation.9 | convolution fusion | flops 6045302784 | bytes 16908288 | tf_op jit(solution)/shard_map/dot_general | solution.py:57
  383.5 2.8 copy.27
  386.4 0.0 reduce-scatter.4.cloned.1.call-update
  386.4 47.9 %reduce-scatter.4.cloned.1.call-done = bf16[384,512]{1,0:T(8,128)(2,1)} async-done(((bf16[3072,512]{1,0:T(8,128)(2,1)}), bf16[384,512]{1,0:T(8,128)(2,1)}) %reduce-scatter.4.cloned.1.call-update) | async-done | bytes 393232
  434.3 1.2 copy.28
  435.5 0.8 add_convert_fusion
  (14 shorter events, 0.1 us)
Async XLA Ops:
  6.5 51.9 %all-gather.5.cloned.1.call-start = ((), (), s32[]{:S(2)}) async-start(), calls=%async_computation.1 | async-start | bytes 3538944 | tf_op jit(solution)/shard_map/all_gather | solution.py:19
  7.3 148.3 %all-gather.7.cloned.1.call-start = ((), (), s32[]{:S(2)}) async-start(), calls=%async_computation.2 | async-start | bytes 7299072 | tf_op jit(solution)/shard_map/all_gather | solution.py:28
  8.0 252.3 %all-gather.9.cloned.1.call-start = ((), (), s32[]{:S(2)}) async-start(), calls=%async_computation.3 | async-start | bytes 9732096 | tf_op jit(solution)/shard_map/all_gather | solution.py:34
  8.7 364.7 %all-gather.11.cloned.1.call-start = ((), (), s32[]{:S(2)}) async-start(), calls=%async_computation.4 | async-start | bytes 12165120 | tf_op jit(solution)/shard_map/all_gather | solution.py:59
  10.5 145.0 %copy-start.7 = (f32[3072]{0:T(1024)S(1)}, f32[3072]{0:T(1024)}, u32[]{:S(2)}) copy-start(f32[3072]{0:T(1024)} %param.9) | copy-start | bytes 36868
  10.6 423.7 %reduce-scatter.4.cloned.1.call-start = ((), (), s32[]{:S(2)}) async-start(), calls=%async_computation.5 | async-start | bytes 3538944
  58.4 2.8 copy-start
  61.3 94.3 %copy-start.3 = (f32[512]{0:T(512)}, f32[512]{0:T(512)S(1)}, u32[]{:S(2)}) copy-start(f32[512]{0:T(512)S(1)} %broadcast_multiply_fusion.2) | copy-start | bytes 6148
  62.2 93.3 %copy-start.5 = (f32[512]{0:T(512)}, f32[512]{0:T(512)S(1)}, u32[]{:S(2)}) copy-start(f32[512]{0:T(512)S(1)} %add_rsqrt_fusion.2) | copy-start | bytes 6148
  181.8 1.2 copy-start.1
  183.3 77.0 %copy-start.4 = (f32[512]{0:T(512)S(1)}, f32[512]{0:T(512)}, u32[]{:S(2)}) copy-start(f32[512]{0:T(512)} %copy-done.3) | copy-start | bytes 6148
  183.3 77.0 %copy-start.6 = (f32[512]{0:T(512)S(1)}, f32[512]{0:T(512)}, u32[]{:S(2)}) copy-start(f32[512]{0:T(512)} %copy-done.5) | copy-start | bytes 6148
  386.4 49.2 %copy-start.2 = (bf16[512,384]{1,0:T(8,128)(2,1)S(1)}, bf16[512,384]{1,0:T(8,128)(2,1)}, u32[]{:S(2)}) copy-start(bf16[512,384]{1,0:T(8,128)(2,1)} %param.8) | copy-start | bytes 1179652
Sparse Core Ops, SparseCore 0:
  9.2 49.2 all-gather.4
  61.2 94.2 all-gather.6
  158.3 101.9 all-gather.8
  262.9 110.5 all-gather.10
  386.5 47.7 reduce-scatter.3
where the time goes:
time: 443 us
  waiting for transfers between devices  362 us (82%)
  matrix products  37.1 us (8%)
  local copies, waits for them, and re-layouts  19.3 us (4%)
  between operations  13.3 us (3%)
  other arithmetic  11.4 us (3%)
    all_gather x1, waiting for transfers between devices, local(): lax.all_gather(out_rows, 'fsdp', axis=1, tiled=True)  98.2 us
    all_gather x1, waiting for transfers between devices, local(): lax.all_gather(w_qkv, 'fsdp', axis=0, tiled=True)  93.3 us
    all_gather x1, waiting for transfers between devices, local(): lax.all_gather(w_up, 'fsdp', axis=0, tiled=True)  72.3 us
    unnamed x6, waiting for transfers between devices  50 us
    all_gather x1, waiting for transfers between devices, local(): panels = lax.all_gather(tokens, 'mp', axis=1, tiled=True)  47.8 us
    dot_general x1, matrix products, local(): jnp.dot(columns, lax.all_gather(w_up, 'fsdp', axis=0, tiled=True), prefer...  14.9 us
    dot_general x1, matrix products, local(): jnp.dot(joined, lax.all_gather(out_rows, 'fsdp', axis=1, tiled=True), pre...  10.1 us
  transfers between devices with their start and end apart: 5, of which 5 were waited for; matrix products, arithmetic and copies ran while one was open for 12% of the time, Pallas kernels for 0%

commit v1 on v0

--- a/solution.py
+++ b/solution.py
@@ -56,7 +56,9 @@
     out_rows = jnp.concatenate([w_proj, w_down], axis=0)
     terms = jnp.dot(
         joined,
-        lax.all_gather(out_rows, "fsdp", axis=1, tiled=True),
+        jnp.concatenate(
+            lax.all_to_all(jnp.stack([out_rows] * lax.axis_size("fsdp")), "fsdp", 0, 0), axis=1
+        ),
         preferred_element_type=jnp.float32,
     )
     branches = lax.psum_scatter(

time: 443 us -> 476 us (1.074)
  waiting for transfers between devices: 362 us -> 376 us
  starting transfers between devices: 0.16 us -> 11.8 us
  local copies, waits for them, and re-layouts: 19.3 us -> 27 us
    all_gather x1 -> x0, waiting for transfers between devices: 98.2 us -> none  [local(): lax.all_gather(out_rows, 'fsdp', axis=1, tiled=True)]
    all_gather x1, waiting for transfers between devices: 93.3 us -> 182 us  [local(): lax.all_gather(w_qkv, 'fsdp', axis=0, tiled=True)]
    all_gather x1, waiting for transfers between devices: 72.3 us -> 103 us  [local(): lax.all_gather(w_up, 'fsdp', axis=0, tiled=True)]
    all_to_all x0 -> x1, starting transfers between devices: none -> 11.6 us  [local(): lax.all_to_all(jnp.stack([out_rows] * lax.axis_size('fsdp')), 'fsdp', 0, 0)]
    all_gather x1, waiting for transfers between devices: 47.8 us -> 41.6 us  [local(): panels = lax.all_gather(tokens, 'mp', axis=1, tiled=True)]
    another operation x0 -> x1, local copies, waits for them, and re-layouts: none -> 5.08 us  [local(): jnp.stack([out_rows] * lax.axis_size('fsdp'))]
    unnamed x6 -> x5, waiting for transfers between devices: 50 us -> 49.5 us
  transfers between devices with their start and end apart: 5 -> 5, of which waited for: 5 -> 4; matrix products, arithmetic and copies ran while one was open for 12% -> 12% of each run, Pallas kernels for 0% -> 0%
where the time goes in v1:
time: 476 us
  waiting for transfers between devices  376 us (79%)
  matrix products  37.1 us (8%)
  local copies, waits for them, and re-layouts  27 us (6%)
  between operations  13.3 us (3%)
  starting transfers between devices  11.8 us (2%)
  other arithmetic  10.7 us (2%)
    all_gather x1, waiting for transfers between devices, local(): lax.all_gather(w_qkv, 'fsdp', axis=0, tiled=True)  182 us
    all_gather x1, waiting for transfers between devices, local(): lax.all_gather(w_up, 'fsdp', axis=0, tiled=True)  103 us
    unnamed x5, waiting for transfers between devices  49.5 us
    all_gather x1, waiting for transfers between devices, local(): panels = lax.all_gather(tokens, 'mp', axis=1, tiled=True)  41.6 us
    dot_general x1, matrix products, local(): jnp.dot(columns, lax.all_gather(w_up, 'fsdp', axis=0, tiled=True), prefer...  15 us
    all_to_all x1, starting transfers between devices, local(): lax.all_to_all(jnp.stack([out_rows] * lax.axis_size('fsdp')), 'fsdp', 0, 0)  11.6 us
    dot_general x1, matrix products, local(): jnp.dot(joined, jnp.concatenate(lax.all_to_all(jnp.stack([out_rows] * lax...  10.1 us
  transfers between devices with their start and end apart: 5, of which 4 were waited for; matrix products, arithmetic and copies ran while one was open for 12% of the time, Pallas kernels for 0%

profile of v1, /device:TPU:16, one launch (start us, length us, event | category | flops | bytes accessed | tf_op | source)
XLA Modules:
  0.0 475.8 jit_solution(12995955687785887714)
XLA Ops:
  6.5 0.0 all-gather.4.cloned.1.call-start
  6.5 0.7 all-gather.4.cloned.1.call-update
  7.3 0.0 all-gather.6.cloned.1.call-start
  7.3 0.7 all-gather.6.cloned.1.call-update
  8.0 1.0 pad_maximum_fusion
  9.0 5.1 %stack.2 = bf16[32,1920,96]{1,2,0:T(8,128)(2,1)} broadcast(bf16[1920,96]{0,1:T(8,128)(2,1)S(1)} %pad_maximum_fusion), dimensions={1,2} | broadcast | bytes 12165120 | tf_op jit(solution)/shard_map/stack | solution.py:60
  14.1 11.6 %all-to-all-start = ((bf16[32,1920,96]{1,2,0:T(8,128)(2,1)}), bf16[32,1920,96]{1,2,0:T(8,128)(2,1)}, u32[]{:S(2)}, u32[]{:S(2)}) async-start(bf16[32,1920,96]{1,2,0:T(8,128)(2,1)} %stack.2), calls=%async_computation | async-start | bytes 23592960 | tf_op jit(solution)/shard_map/all_to_all | solution.py:60
  25.7 0.0 all-gather.8.cloned.1.call-start
  25.8 0.0 copy-start.6
  25.8 0.7 all-gather.8.cloned.1.call-update
  26.5 0.0 reduce-scatter.4.cloned.1.call-start
  26.5 41.6 %all-gather.4.cloned.1.call-done = bf16[512,3072]{1,0:T(8,128)(2,1)} async-done(((bf16[512,384]{1,0:T(8,128)(2,1)}), bf16[512,3072]{1,0:T(8,128)(2,1)}) %all-gather.4.cloned.1.call-update) | async-done | bytes 3145744 | tf_op jit(solution)/shard_map/all_gather | solution.py:19
  68.2 2.5 convert_reduce_fusion
  70.7 0.3 copy-done
  71.0 1.0 fusion.3
  72.0 182.0 %all-gather.6.cloned.1.call-done = bf16[3072,3,384]{2,0,1:T(8,128)(2,1)} async-done(((bf16[96,3,384]{2,0,1:T(8,128)(2,1)}), bf16[3072,3,384]{2,0,1:T(8,128)(2,1)}) %all-gather.6.cloned.1.call-update) | async-done | bytes 7077904 | tf_op jit(solution)/shard_map/all_gather | solution.py:28
  254.0 0.0 copy-done.6
  254.0 7.1 %fusion.21 = f32[3,512,384]{1,2,0:T(8,128)S(1)} fusion(bf16[3072,3,384]{2,0,1:T(8,128)(2,1)} %all-gather.6.cloned.1.call-done, bf16[512,3072]{1,0:T(8,128)(2,1)S(1)} %copy-done, f32[3072]{0:T(1024)S(1)} %copy-done.6, f32[512]{0:T(512)S(1)} %add_rsqrt_fusion.2, f32[512]{0:T(512)S(1)} %broadcast_multiply_fusion.2), kind=kOutput, calls=%fused_computation.33 | convolution fusion | flops 3631742976 | bytes 12599296 | tf_op jit(solution)/shard_map/td,dca->cta/dot_general | solution.py:25
  261.1 0.0 copy-start.2
  261.1 1.4 copy-done.2
  262.5 0.8 convert_element_type.46
  263.4 2.6 fusion.41
  266.0 2.5 reshape_squeeze.13
  268.5 2.5 reshape_squeeze.11
  271.0 1.2 reduce_sum.65
  272.2 1.2 reduce_sum.67
  273.4 2.3 copy.21
  275.7 2.1 copy.20
  277.8 1.3 multiply_reduce_fusion.1
  279.1 1.3 multiply_reduce_fusion
  280.4 0.0 copy-done.4
  280.5 0.0 copy-done.5
  280.5 2.4 convolution_multiply_fusion
  282.9 0.0 copy-start.1
  282.9 1.1 copy-done.1
  284.0 0.3 fusion.42
  284.3 2.5 fusion.26
  286.9 1.1 copy.27
  287.9 1.1 copy.35
  289.0 102.8 %all-gather.8.cloned.1.call-done = bf16[3072,1536]{1,0:T(8,128)(2,1)} async-done(((bf16[96,1536]{1,0:T(8,128)(2,1)}), bf16[3072,1536]{1,0:T(8,128)(2,1)}) %all-gather.8.cloned.1.call-update) | async-done | bytes 9437200 | tf_op jit(solution)/shard_map/all_gather | solution.py:34
  391.9 15.0 %fusion.8 = bf16[512,1536]{1,0:T(8,128)(2,1)} fusion(bf16[3072,1536]{1,0:T(8,128)(2,1)} %all-gather.8.cloned.1.call-done, bf16[512,3072]{1,0:T(8,128)(2,1)S(1)} %copy-done, f32[3072]{0:T(1024)} %param.9, f32[512]{0:T(512)S(1)} %add_rsqrt_fusion.2, f32[512]{0:T(512)S(1)} %broadcast_multiply_fusion.2), kind=kOutput, calls=%fused_computation.12 | convolution fusion | flops 4890820608 | bytes 14172160 | tf_op jit(solution)/shard_map/dot_general | solution.py:32
  406.9 0.0 all-to-all-done
  406.9 10.1 %convolution_convert_fusion = bf16[512,3072]{1,0:T(8,128)(2,1)S(1)} fusion(bf16[1920,3072]{0,1:T(8,128)(2,1)} %bitcast.10, bf16[512,1536]{1,0:T(8,128)(2,1)} %fusion.8, bf16[512,384]{1,0:T(8,128)(2,1)S(1)} %bitcast.42), kind=kOutput, calls=%fused_computation.9 | convolution fusion | flops 6045302784 | bytes 16908288 | tf_op jit(solution)/shard_map/dot_general | solution.py:57
  416.9 2.8 copy.28
  419.7 0.0 reduce-scatter.4.cloned.1.call-update
  419.8 47.4 %reduce-scatter.4.cloned.1.call-done = bf16[384,512]{1,0:T(8,128)(2,1)} async-done(((bf16[3072,512]{1,0:T(8,128)(2,1)}), bf16[384,512]{1,0:T(8,128)(2,1)}) %reduce-scatter.4.cloned.1.call-update) | async-done | bytes 393232
  467.2 1.2 copy.29
  468.4 0.8 add_convert_fusion
  (12 shorter events, 0.1 us)
Async XLA Ops:
  6.5 61.6 %all-gather.4.cloned.1.call-start = ((), (), s32[]{:S(2)}) async-start(), calls=%async_computation.2 | async-start | bytes 3538944 | tf_op jit(solution)/shard_map/all_gather | solution.py:19
  7.3 246.7 %all-gather.6.cloned.1.call-start = ((), (), s32[]{:S(2)}) async-start(), calls=%async_computation.3 | async-start | bytes 7299072 | tf_op jit(solution)/shard_map/all_gather | solution.py:28
  14.1 392.8 %all-to-all-start = ((bf16[32,1920,96]{1,2,0:T(8,128)(2,1)}), bf16[32,1920,96]{1,2,0:T(8,128)(2,1)}, u32[]{:S(2)}, u32[]{:S(2)}) async-start(bf16[32,1920,96]{1,2,0:T(8,128)(2,1)} %stack.2), calls=%async_computation | async-start | bytes 23592960 | tf_op jit(solution)/shard_map/all_to_all | solution.py:60
  25.7 366.1 %all-gather.8.cloned.1.call-start = ((), (), s32[]{:S(2)}) async-start(), calls=%async_computation.4 | async-start | bytes 9732096 | tf_op jit(solution)/shard_map/all_gather | solution.py:34
  25.8 228.2 %copy-start.6 = (f32[3072]{0:T(1024)S(1)}, f32[3072]{0:T(1024)}, u32[]{:S(2)}) copy-start(f32[3072]{0:T(1024)} %param.9) | copy-start | bytes 36868
  26.5 440.7 %reduce-scatter.4.cloned.1.call-start = ((), (), s32[]{:S(2)}) async-start(), calls=%async_computation.5 | async-start | bytes 3538944
  68.2 2.8 copy-start
  261.1 1.4 copy-start.2
  271.0 9.5 %copy-start.4 = (f32[3,128]{1,0:T(4,128)S(1)}, f32[3,128]{1,0:T(4,128)}, u32[]{:S(2)}) copy-start(f32[3,128]{1,0:T(4,128)} %param.13) | copy-start | bytes 4612
  271.0 9.5 %copy-start.5 = (f32[3,128]{1,0:T(4,128)S(1)}, f32[3,128]{1,0:T(4,128)}, u32[]{:S(2)}) copy-start(f32[3,128]{1,0:T(4,128)} %param.12) | copy-start | bytes 4612
  282.9 1.2 copy-start.1
  419.7 48.6 %copy-start.3 = (bf16[512,384]{1,0:T(8,128)(2,1)S(1)}, bf16[512,384]{1,0:T(8,128)(2,1)}, u32[]{:S(2)}) copy-start(bf16[512,384]{1,0:T(8,128)(2,1)} %param.8) | copy-start | bytes 1179652
Sparse Core Ops, SparseCore 0:
  9.2 58.9 all-gather.3
  71.0 182.9 all-gather.5
  256.8 135.0 all-gather.7
  419.9 47.2 reduce-scatter.3
